TPU v7x, 32 devices: a whole 2x2x4 slice. The times are simulated.
32 devices in a mesh: src: 8 (over y, x, core), tm: 4 (over z).
Axes of the slice: x: 2, y: 2, z: 4, core: 2. Of those that a mesh axis runs over, the one named last changes fastest.
Arguments:
- attitude_design: float32 [4, 131072], P(None, ('src', 'tm')), may hold values from -6 to 6
- source_design: float32 [5, 131072], P(None, ('src', 'tm')), may hold values from -6 to 6
- scan_phase: float32 [131072], P(('src', 'tm')), may hold values from 0 to 1
- obs_weight: float32 [131072], P(('src', 'tm')), may hold values from 0.25 to 4
- obs_residual: float32 [131072], P(('src', 'tm')), may hold values from -6 to 6
- source_id: int32 [131072], P(('src', 'tm')), may hold values from 0 to 2047
- knot_start: int32 [131072], P(('src', 'tm')), may hold values from 0 to 1023
- time_segment: int32 [131072, 1], P(('src', 'tm')), may hold values from 0 to 3; in each aligned block of 4096 rows (0 to 4095, 4096 to 8191, ...) at most 2048 rows name the same one
Outputs:
- source_update: float32 [5, 16384], P(None, 'src')
- attitude_update: float32 [4, 4096], P(None, 'tm')
Inputs may be any that keep to these rules, and one draw needn't show every extreme that they name: `time_segment`: among the observations of one device, at most 2048 fall in any one time segment, and in some device some segment receives exactly 2048.
All inputs are finite; a program needn't handle non-finite values.
Results may differ from a plain program's by a relative error of at most 0.0003.
Values sent between devices are 32-bit elements; how exact they have to be, the bound alone decides.
A program may use at most 64 MiB of HBM per device.

v0:
```python
import jax
import jax.numpy as jnp
from jax import lax
from jax.sharding import PartitionSpec as P

KS = 1024
S_DEV = 2048
ITERS = 4
prior_source = 1.0
prior_attitude = 1.0
index_pairs = [(i, j) for i in range(5) for j in range(i, 5)]
spline_pairs = [(j, d) for d in range(4) for j in range(4 - d)]
component_pairs = [(c, e) for c in range(4) for e in range(c, 4)]


def from_behind(x, axis, by):
    count = lax.axis_size(axis)
    pairs = [(i, i + by) for i in range(count) if 0 <= i + by < count]
    return lax.ppermute(x, axis, pairs)


def with_halo(cells, sides, width):
    for axis, dim in sides:
        count = lax.axis_size(axis)
        ends = count - 1
        head = lax.slice_in_dim(cells, 0, width, axis=dim)
        tail = lax.slice_in_dim(cells, cells.shape[dim] - width, cells.shape[dim], axis=dim)
        cells = jnp.concatenate(
            [
                lax.ppermute(tail, axis, [(i, (i + 1) % count) for i in range(ends)]),
                cells,
                lax.ppermute(head, axis, [((i + 1) % count, i) for i in range(ends)]),
            ],
            axis=dim,
        )
    return cells


def spline_weights(fraction):
    rest = 1.0 - fraction
    square = fraction * fraction
    cube = square * fraction
    return [
        rest * rest * rest / 6.0,
        (3.0 * cube - 6.0 * square + 4.0) / 6.0,
        (-3.0 * cube + 3.0 * square + 3.0 * fraction + 1.0) / 6.0,
        cube / 6.0,
    ]


def knot_features(attitude, fraction, weights, reduced):
    basis = spline_weights(fraction)
    outer = [attitude[c] * attitude[e] for c, e in component_pairs]
    rows = []
    for j, d in spline_pairs:
        factor = weights * basis[j] * basis[j + d]
        for product in outer:
            rows.append(factor * product)
    for j in range(4):
        factor = weights * basis[j] * reduced
        for c in range(4):
            rows.append(factor * attitude[c])
    filler = jnp.zeros_like(fraction)
    while len(rows) < 128:
        rows.append(filler)
    return jnp.stack(rows, 0)


def collect(features, index, count):
    n_rows = index.shape[0]
    block = min(512, n_rows)
    steps = n_rows // block
    width = features.shape[0]
    feat_blocks = jnp.transpose(features.reshape(width, steps, block), (1, 0, 2))
    index_blocks = index.reshape(steps, block)
    columns = jnp.arange(count, dtype=jnp.int32)

    def add_block(total, pieces):
        feat, idx = pieces
        onehot = (idx[:, None] == columns[None, :]).astype(jnp.float32)
        return (
            total
            + jnp.dot(
                feat, onehot, precision=lax.Precision.HIGHEST, preferred_element_type=jnp.float32
            ),
            None,
        )

    total, _ = lax.scan(
        add_block, jnp.zeros((width, count), jnp.float32), (feat_blocks, index_blocks)
    )
    return total


def band_from(collected, count_out):
    padded = jnp.pad(collected, ((0, 0), (3, 3)))
    rows = []
    for d in range(4):
        for c in range(4):
            for e in range(4):
                q = component_pairs.index((min(c, e), max(c, e)))
                total = None
                for j in range(4 - d):
                    p = spline_pairs.index((j, d))
                    term = padded[p * 10 + q, 3 - j : 3 - j + count_out]
                    total = term if total is None else total + term
                rows.append(total)
    for c in range(4):
        total = None
        for j in range(4):
            term = padded[100 + 4 * j + c, 3 - j : 3 - j + count_out]
            total = term if total is None else total + term
        rows.append(total)
    return jnp.stack(rows, 0)


def source_rows(design, weights, resid):
    pieces = [weights * design[i] * design[j] for i, j in index_pairs]
    pieces = pieces + [weights * design[i] * resid for i in range(5)]
    return jnp.stack(pieces, 0)


def pick_sources(source_update, source_id):
    n_rows = source_id.shape[0]
    block = min(512, n_rows)
    steps = n_rows // block
    columns = jnp.arange(source_update.shape[1], dtype=jnp.int32)

    def pick_block(idx):
        onehot = (idx[:, None] == columns[None, :]).astype(jnp.float32)
        return lax.dot_general(
            source_update,
            onehot,
            (((1,), (1,)), ((), ())),
            precision=lax.Precision.HIGHEST,
            preferred_element_type=jnp.float32,
        )

    picked = lax.map(pick_block, source_id.reshape(steps, block))
    return jnp.transpose(picked, (1, 0, 2)).reshape(5, n_rows)


def solve_five(normals):
    entry = {}
    for n, (i, j) in enumerate(index_pairs):
        entry[j, i] = normals[n]
    for i in range(5):
        entry[i, i] = entry[i, i] + prior_source
    lower = {}
    for i in range(5):
        for j in range(i + 1):
            value = entry[i, j]
            for k in range(j):
                value = value - lower[i, k] * lower[j, k]
            if i == j:
                lower[i, i] = jnp.sqrt(value)
            else:
                lower[i, j] = value / lower[j, j]
    forward = []
    for i in range(5):
        value = normals[15 + i]
        for k in range(i):
            value = value - lower[i, k] * forward[k]
        forward.append(value / lower[i, i])
    solution = [None] * 5
    for i in range(4, -1, -1):
        value = forward[i]
        for k in range(i + 1, 5):
            value = value - lower[k, i] * solution[k]
        solution[i] = value / lower[i, i]
    return jnp.stack(solution, 0)


def apply_band(matrix, matrix_ext, padded, columns):
    result = prior_attitude * padded[:, 3 : 3 + columns]
    for d in range(4):
        block_mat = matrix[16 * d : 16 * d + 16].reshape(4, 4, columns)
        result = result + jnp.einsum(
            "abk,bk->ak",
            block_mat,
            padded[:, 3 + d : 3 + d + columns],
            precision=lax.Precision.HIGHEST,
        )
    for d in range(1, 4):
        block_mat = matrix_ext[16 * d : 16 * d + 16, 3 - d : 3 - d + columns].reshape(4, 4, columns)
        result = result + jnp.einsum(
            "bak,bk->ak",
            block_mat,
            padded[:, 3 - d : 3 - d + columns],
            precision=lax.Precision.HIGHEST,
        )
    return result


def body(
    attitude_design,
    source_design,
    scan_phase,
    obs_weight,
    obs_residual,
    source_id,
    knot_start,
    time_segment,
):
    contrib = source_rows(source_design, obs_weight, obs_residual)
    own_normals = collect(contrib, source_id, S_DEV)
    normals = lax.psum(own_normals, "tm")
    source_update = solve_five(normals)
    picked = pick_sources(source_update, source_id)
    reduced = obs_residual - jnp.sum(source_design * picked, axis=0)
    segment_of = time_segment[:, 0]
    seg_count = lax.axis_size("tm")
    knot_count = KS * seg_count
    width = KS
    features = knot_features(attitude_design, scan_phase, obs_weight, reduced)
    first = segment_of * KS + knot_start
    full_band = band_from(collect(features, first, knot_count), knot_count)
    partial_band = lax.psum_scatter(full_band, "tm", scatter_dimension=1, tiled=True)
    band = lax.psum(partial_band, "src")
    matrix = band[:64]
    rhs = band[64:68]
    rim = from_behind(matrix[:, width - 3 :], "tm", 1)
    matrix_ext = jnp.concatenate([rim, matrix], 1)

    def squares(resid):
        return lax.psum(jnp.sum(resid * resid), "tm")

    solution = jnp.zeros_like(rhs)
    resid = rhs
    direction = rhs
    norm_now = squares(resid)
    for step in range(ITERS):
        padded = with_halo(direction, (("tm", 1),), 3)
        image = apply_band(matrix, matrix_ext, padded, width)
        alpha = norm_now / lax.psum(jnp.sum(direction * image), "tm")
        solution = solution + alpha * direction
        resid = resid - alpha * image
        norm_next = squares(resid)
        direction = resid + norm_next / norm_now * direction
        norm_now = norm_next
    return (source_update, solution)


def solution(mesh):
    in_specs = (
        P(None, ("src", "tm")),
        P(None, ("src", "tm")),
        P(("src", "tm")),
        P(("src", "tm")),
        P(("src", "tm")),
        P(("src", "tm")),
        P(("src", "tm")),
        P(("src", "tm"), None),
    )
    out_specs = (P(None, "src"), P(None, "tm"))
    return jax.shard_map(body, mesh=mesh, in_specs=in_specs, out_specs=out_specs, check_vma=False)
```

profile of v0, /device:TPU:0, one launch (start us, length us, event | category | flops | bytes accessed | tf_op | source)
XLA Modules:
  0.0 381.2 jit_solution(8686215331941736714)
XLA Ops:
  10.7 12.4 %while.34 = (s32[]{:T(128)}, f32[20,2048]{1,0:T(8,128)S(1)}, f32[8,20,512]{2,1,0:T(8,128)S(1)}, s32[8,512]{1,0:T(8,128)S(1)}, s32[]{:T(128)}, /*index=5*/s32[]{:T(128)}) while((s32[]{:T(128)}, f32[20,2048]{1,0:T(8,128)S(1)}, f32[8,20,512]{2,1,0:T(8,128)S(1)}, s32[8,512]{1,0:T(8,128)S(1)}, s32[]{:T(128)}, ...), condition=%wide.region_1.2_spmd.clone, body=%wide.region_0.1_spmd.clone.sunk | while | flops 252788736 | bytes 415831 | solution.py:89
  24.8 36.7 %all-reduce.5.cloned.1.call-done = f32[20,2048]{1,0:T(8,128)} async-done(((f32[20,2048]{1,0:T(8,128)}), f32[20,2048]{1,0:T(8,128)}) %all-reduce.5.cloned.1.call-update) | async-done | bytes 163856 | tf_op jit(solution)/shard_map/psum | solution.py:207
  65.8 16.3 %while.33 = (s32[]{:T(128)}, f32[8,5,512]{2,1,0:T(8,128)S(1)}, s32[8,512]{1,0:T(8,128)S(1)}, f32[5,2048]{1,0:T(8,128)S(1)}, s32[]{:T(128)}) while((s32[]{:T(128)}, f32[8,5,512]{2,1,0:T(8,128)S(1)}, s32[8,512]{1,0:T(8,128)S(1)}, f32[5,2048]{1,0:T(8,128)S(1)}, s32[]{:T(128)}) %tuple.351), condition=%wide.region_4.5_spmd.clone, body=%wide.region_3.4_spmd.clone.sunk | while | flops 63963136 | bytes 88133 | solution.py:139
  69.8 2.0 fusion.158
  71.9 2.0 fusion.158
  73.9 2.0 fusion.158
  78.0 2.0 fusion.158
  84.6 24.5 %stack.624 = f32[128,8,512]{2,0,1:T(8,128)} concatenate(f32[1,8,512]{2,0,1:T(1,128)S(1)} %bitcast.483, f32[1,8,512]{2,0,1:T(1,128)} %bitcast.534, f32[1,8,512]{2,0,1:T(1,128)} %bitcast.535, f32[1,8,512]{2,0,1:T(1,128)} %bitcast.536, f32[1,8,512]{2,0,1:T(1,128)S(1)} %bitcast.485, f32[1,8,512]{2,0,1:T(1,128)} %bitcast.537, f32[1,8,512]{2,0,1:T(1,128)} %bitcast.538, ...), dimensions={0} | concatenate | bytes 4194304 | tf_op jit(solution)/shard_map/stack | solution.py:66
  109.1 45.1 %while.35 = (s32[]{:T(128)}, f32[128,4096]{1,0:T(8,128)S(1)}, f32[8,128,512]{2,1,0:T(8,128)}, s32[8,512]{1,0:T(8,128)}, s32[]{:T(128)}, /*index=5*/s32[]{:T(128)}) while((s32[]{:T(128)}, f32[128,4096]{1,0:T(8,128)S(1)}, f32[8,128,512]{2,1,0:T(8,128)}, s32[8,512]{1,0:T(8,128)}, s32[]{:T(128)}, /*index=5*/s32[]{:T(128)}) %tuple.349), condition=%wide.region_7.8_spmd.clone, body=%wide.region_6.7_spmd.clone.sunk | while | flops 3224371200 | bytes 4463187 | solution.py:89
  109.8 4.9 %fusion.162 = f32[128,4096]{1,0:T(8,128)S(1)} fusion(s32[512]{0:T(512)S(1)} %bitcast.579, f32[128,4096]{1,0:T(8,128)S(1)} %get-tuple-element.605, pred[]{:T(512)S(6)} %compare.8, f32[8,128,512]{2,1,0:T(8,128)} %get-tuple-element.612, s32[]{:T(128)} %get-tuple-element.604), kind=kOutput, calls=%fused_computation.19.clone.1 | convolution fusion | flops 3224371200 | bytes 4459009 | tf_op jit(solution)/shard_map/while/body/eval_jaxpr/dot_general | solution.py:83
  115.4 4.9 %fusion.162 = f32[128,4096]{1,0:T(8,128)S(1)} fusion(s32[512]{0:T(512)S(1)} %bitcast.579, f32[128,4096]{1,0:T(8,128)S(1)} %get-tuple-element.605, pred[]{:T(512)S(6)} %compare.8, f32[8,128,512]{2,1,0:T(8,128)} %get-tuple-element.612, s32[]{:T(128)} %get-tuple-element.604), kind=kOutput, calls=%fused_computation.19.clone.1 | convolution fusion | flops 3224371200 | bytes 4459009 | tf_op jit(solution)/shard_map/while/body/eval_jaxpr/dot_general | solution.py:83
  121.1 4.9 %fusion.162 = f32[128,4096]{1,0:T(8,128)S(1)} fusion(s32[512]{0:T(512)S(1)} %bitcast.579, f32[128,4096]{1,0:T(8,128)S(1)} %get-tuple-element.605, pred[]{:T(512)S(6)} %compare.8, f32[8,128,512]{2,1,0:T(8,128)} %get-tuple-element.612, s32[]{:T(128)} %get-tuple-element.604), kind=kOutput, calls=%fused_computation.19.clone.1 | convolution fusion | flops 3224371200 | bytes 4459009 | tf_op jit(solution)/shard_map/while/body/eval_jaxpr/dot_general | solution.py:83
  126.7 4.9 %fusion.162 = f32[128,4096]{1,0:T(8,128)S(1)} fusion(s32[512]{0:T(512)S(1)} %bitcast.579, f32[128,4096]{1,0:T(8,128)S(1)} %get-tuple-element.605, pred[]{:T(512)S(6)} %compare.8, f32[8,128,512]{2,1,0:T(8,128)} %get-tuple-element.612, s32[]{:T(128)} %get-tuple-element.604), kind=kOutput, calls=%fused_computation.19.clone.1 | convolution fusion | flops 3224371200 | bytes 4459009 | tf_op jit(solution)/shard_map/while/body/eval_jaxpr/dot_general | solution.py:83
  132.3 4.9 %fusion.162 = f32[128,4096]{1,0:T(8,128)S(1)} fusion(s32[512]{0:T(512)S(1)} %bitcast.579, f32[128,4096]{1,0:T(8,128)S(1)} %get-tuple-element.605, pred[]{:T(512)S(6)} %compare.8, f32[8,128,512]{2,1,0:T(8,128)} %get-tuple-element.612, s32[]{:T(128)} %get-tuple-element.604), kind=kOutput, calls=%fused_computation.19.clone.1 | convolution fusion | flops 3224371200 | bytes 4459009 | tf_op jit(solution)/shard_map/while/body/eval_jaxpr/dot_general | solution.py:83
  137.9 4.9 %fusion.162 = f32[128,4096]{1,0:T(8,128)S(1)} fusion(s32[512]{0:T(512)S(1)} %bitcast.579, f32[128,4096]{1,0:T(8,128)S(1)} %get-tuple-element.605, pred[]{:T(512)S(6)} %compare.8, f32[8,128,512]{2,1,0:T(8,128)} %get-tuple-element.612, s32[]{:T(128)} %get-tuple-element.604), kind=kOutput, calls=%fused_computation.19.clone.1 | convolution fusion | flops 3224371200 | bytes 4459009 | tf_op jit(solution)/shard_map/while/body/eval_jaxpr/dot_general | solution.py:83
  143.5 4.9 %fusion.162 = f32[128,4096]{1,0:T(8,128)S(1)} fusion(s32[512]{0:T(512)S(1)} %bitcast.579, f32[128,4096]{1,0:T(8,128)S(1)} %get-tuple-element.605, pred[]{:T(512)S(6)} %compare.8, f32[8,128,512]{2,1,0:T(8,128)} %get-tuple-element.612, s32[]{:T(128)} %get-tuple-element.604), kind=kOutput, calls=%fused_computation.19.clone.1 | convolution fusion | flops 3224371200 | bytes 4459009 | tf_op jit(solution)/shard_map/while/body/eval_jaxpr/dot_general | solution.py:83
  149.1 4.9 %fusion.162 = f32[128,4096]{1,0:T(8,128)S(1)} fusion(s32[512]{0:T(512)S(1)} %bitcast.579, f32[128,4096]{1,0:T(8,128)S(1)} %get-tuple-element.605, pred[]{:T(512)S(6)} %compare.8, f32[8,128,512]{2,1,0:T(8,128)} %get-tuple-element.612, s32[]{:T(128)} %get-tuple-element.604), kind=kOutput, calls=%fused_computation.19.clone.1 | convolution fusion | flops 3224371200 | bytes 4459009 | tf_op jit(solution)/shard_map/while/body/eval_jaxpr/dot_general | solution.py:83
  157.2 7.2 %stack.625 = f32[68,4096]{1,0:T(8,128)} concatenate(f32[1,4096]{1,0:T(1,128)S(1)} %get-tuple-element.269, f32[1,4096]{1,0:T(1,128)S(1)} %get-tuple-element.268, f32[1,4096]{1,0:T(1,128)S(1)} %get-tuple-element.267, f32[1,4096]{1,0:T(1,128)S(1)} %get-tuple-element.266, f32[1,4096]{1,0:T(1,128)S(1)} %get-tuple-element.268, f32[1,4096]{1,0:T(1,128)S(1)} %get-tuple-element.265, ...), dimensions={0} | concatenate | bytes 2228224 | tf_op jit(solution)/shard_map/stack | solution.py:114
  164.5 29.0 %reduce-scatter.2.cloned.1.call-done = f32[68,1024]{1,0:T(8,128)} async-done(((f32[68,4096]{1,0:T(8,128)}), f32[68,1024]{1,0:T(8,128)}) %reduce-scatter.2.cloned.1.call-update) | async-done | bytes 278544 | tf_op jit(solution)/shard_map/reduce_scatter | solution.py:218
  193.5 55.2 %all-reduce.7.cloned.1.call-done = f32[68,1024]{1,0:T(8,128)} async-done(((f32[68,1024]{1,0:T(8,128)}), f32[68,1024]{1,0:T(8,128)}) %all-reduce.7.cloned.1.call-update) | async-done | bytes 278544 | tf_op jit(solution)/shard_map/psum | solution.py:219
  250.9 4.5 %collective-permute-start.1 = (f32[4,3]{1,0:T(4,128)S(1)}, f32[4,3]{1,0:T(4,128)S(1)}, u32[]{:S(2)}, u32[]{:S(2)}) collective-permute-start(f32[4,3]{1,0:T(4,128)S(1)} %get-tuple-element.277), channel_id=1, source_target_pairs={{0,1},{1,2},{2,3},{4,5},{5,6},{6,7},{8,9},{9,10},{10,11},{12,13},{... | collective-permute-start | bytes 152 | tf_op jit(solution)/shard_map/ppermute | solution.py:30
  257.3 3.4 collective-permute-start.2
  263.3 11.7 %all-reduce.1 = (f32[]{:T(128)}, f32[]{:T(128)}) all-reduce(f32[]{:T(128)} %get-tuple-element.131, f32[]{:T(128)} %get-tuple-element.130), channel_id=1, replica_groups=mesh['src'=8,'tm'=4] {'tm'}, use_global_device_ids=true, to_apply=%region_11.12 | all-reduce | flops 2 | bytes 16 | tf_op jit(solution)/shard_map/psum | solution.py:226
  276.8 9.3 %psum.74 = f32[]{:T(128)} all-reduce(f32[]{:T(128)} %multiply_reduce_fusion.33), channel_id=1, replica_groups=mesh['src'=8,'tm'=4] {'tm'}, use_global_device_ids=true, to_apply=%region_15.16 | all-reduce | flops 1 | bytes 8 | tf_op jit(solution)/shard_map/psum | solution.py:226
  288.8 4.5 %collective-permute-start.4 = (f32[4,3]{1,0:T(4,128)S(1)}, f32[4,3]{1,0:T(4,128)S(1)}, u32[]{:S(2)}, u32[]{:S(2)}) collective-permute-start(f32[4,3]{1,0:T(4,128)S(1)} %get-tuple-element.417), channel_id=1, source_target_pairs={{0,1},{1,2},{2,3},{4,5},{5,6},{6,7},{8,9},{9,10},{10,11},{12,13},{... | collective-permute-start | bytes 152 | tf_op jit(solution)/shard_map/ppermute | solution.py:30
  295.7 11.8 %psum.75 = f32[]{:T(128)} all-reduce(f32[]{:T(128)} %get-tuple-element.162), channel_id=1, replica_groups=mesh['src'=8,'tm'=4] {'tm'}, use_global_device_ids=true, to_apply=%region_17.18 | all-reduce | flops 1 | bytes 8 | tf_op jit(solution)/shard_map/psum | solution.py:235
  309.4 9.2 %psum.76 = f32[]{:T(128)} all-reduce(f32[]{:T(128)} %get-tuple-element.160), channel_id=1, replica_groups=mesh['src'=8,'tm'=4] {'tm'}, use_global_device_ids=true, to_apply=%region_19.20 | all-reduce | flops 1 | bytes 8 | tf_op jit(solution)/shard_map/psum | solution.py:226
  321.3 4.5 %collective-permute-start.6 = (f32[4,3]{1,0:T(4,128)S(1)}, f32[4,3]{1,0:T(4,128)S(1)}, u32[]{:S(2)}, u32[]{:S(2)}) collective-permute-start(f32[4,3]{1,0:T(4,128)S(1)} %get-tuple-element.412), channel_id=1, source_target_pairs={{0,1},{1,2},{2,3},{4,5},{5,6},{6,7},{8,9},{9,10},{10,11},{12,13},{... | collective-permute-start | bytes 152 | tf_op jit(solution)/shard_map/ppermute | solution.py:30
  328.2 11.9 %psum.77 = f32[]{:T(128)} all-reduce(f32[]{:T(128)} %get-tuple-element.158), channel_id=1, replica_groups=mesh['src'=8,'tm'=4] {'tm'}, use_global_device_ids=true, to_apply=%region_21.22 | all-reduce | flops 1 | bytes 8 | tf_op jit(solution)/shard_map/psum | solution.py:235
  341.9 9.2 %psum.78 = f32[]{:T(128)} all-reduce(f32[]{:T(128)} %multiply_reduce_fusion.29), channel_id=1, replica_groups=mesh['src'=8,'tm'=4] {'tm'}, use_global_device_ids=true, to_apply=%region_23.24 | all-reduce | flops 1 | bytes 8 | tf_op jit(solution)/shard_map/psum | solution.py:226
  353.8 4.5 %collective-permute-start.8 = (f32[4,3]{1,0:T(4,128)S(1)}, f32[4,3]{1,0:T(4,128)S(1)}, u32[]{:S(2)}, u32[]{:S(2)}) collective-permute-start(f32[4,3]{1,0:T(4,128)S(1)} %get-tuple-element.407), channel_id=1, source_target_pairs={{0,1},{1,2},{2,3},{4,5},{5,6},{6,7},{8,9},{9,10},{10,11},{12,13},{... | collective-permute-start | bytes 152 | tf_op jit(solution)/shard_map/ppermute | solution.py:30
  360.7 12.0 %psum.79 = f32[]{:T(128)} all-reduce(f32[]{:T(128)} %fusion.71), channel_id=1, replica_groups=mesh['src'=8,'tm'=4] {'tm'}, use_global_device_ids=true, to_apply=%region_25.26 | all-reduce | flops 1 | bytes 8 | tf_op jit(solution)/shard_map/psum | solution.py:235
  (164 shorter events, 61.1 us)
Async XLA Ops:
  7.2 54.3 %all-reduce.5.cloned.1.call-start = ((), (), s32[]{:S(2)}) async-start(), calls=%async_computation.1 | async-start | bytes 393216 | tf_op jit(solution)/shard_map/psum | solution.py:207
  10.7 13.3 %copy-start.4 = (f32[4,4096]{1,0:T(4,128)S(1)}, f32[4,4096]{1,0:T(4,128)}, u32[]{:S(2)}) copy-start(f32[4,4096]{1,0:T(4,128)} %param.14) | copy-start | bytes 196612
  10.7 13.4 %copy-start.9 = (s32[4096,1]{0,1:T(1,128)S(1)}, s32[4096,1]{0,1:T(1,128)}, u32[]{:S(2)}) copy-start(s32[4096,1]{0,1:T(1,128)} %param.21) | copy-start | bytes 49156
  10.7 13.4 %copy-start.8 = (s32[4096]{0:T(1024)S(1)}, s32[4096]{0:T(1024)}, u32[]{:S(2)}) copy-start(s32[4096]{0:T(1024)} %param.20) | copy-start | bytes 49156
  23.1 0.7 copy-start.2
  23.8 169.7 %reduce-scatter.2.cloned.1.call-start = ((), (), s32[]{:S(2)}) async-start(), calls=%async_computation.2 | async-start | bytes 1474560 | tf_op jit(solution)/shard_map/reduce_scatter | solution.py:218
  65.7 16.3 %copy-start.1 = (f32[5,4096]{1,0:T(8,128)S(1)}, f32[5,4096]{1,0:T(8,128)}, u32[]{:S(2)}) copy-start(f32[5,4096]{1,0:T(8,128)} %param.15) | copy-start | bytes 245764
  65.7 16.4 %copy-start.3 = (f32[4096]{0:T(1024)S(1)}, f32[4096]{0:T(1024)}, u32[]{:S(2)}) copy-start(f32[4096]{0:T(1024)} %param.17) | copy-start | bytes 49156
  65.7 16.4 %copy-start.6 = (f32[4096]{0:T(1024)S(1)}, f32[4096]{0:T(1024)}, u32[]{:S(2)}) copy-start(f32[4096]{0:T(1024)} %param.18) | copy-start | bytes 49156
  65.7 16.4 %copy-start.7 = (f32[4096]{0:T(1024)S(1)}, f32[4096]{0:T(1024)}, u32[]{:S(2)}) copy-start(f32[4096]{0:T(1024)} %param.16) | copy-start | bytes 49156
  82.0 1.4 copy-start.5
  164.5 84.3 %all-reduce.7.cloned.1.call-start = ((), (), s32[]{:S(2)}) async-start(), calls=%async_computation.3 | async-start | bytes 589824 | tf_op jit(solution)/shard_map/psum | solution.py:219
  248.7 13.5 %slice-start = ((f32[68,1024]{1,0:T(8,128)}), f32[64,1024]{1,0:T(8,128)S(1)}, s32[]{:S(2)}) async-start(f32[68,1024]{1,0:T(8,128)} %all-reduce.7.cloned.1.call-done), calls=%async_computation.4 | async-start | bytes 524288 | tf_op jit(solution)/shard_map/slice | solution.py:220
  248.7 13.8 %copy-start = (f32[68,1024]{1,0:T(8,128)S(1)}, f32[68,1024]{1,0:T(8,128)}, u32[]{:S(2)}) copy-start(f32[68,1024]{1,0:T(8,128)} %all-reduce.7.cloned.1.call-done) | copy-start | bytes 835588
  249.6 11.9 %collective-permute-start = (f32[4,3]{1,0:T(4,128)S(1)}, f32[4,3]{1,0:T(4,128)S(1)}, u32[]{:S(2)}, u32[]{:S(2)}) collective-permute-start(f32[4,3]{1,0:T(4,128)S(1)} %get-tuple-element.276), channel_id=1, source_target_pairs={{1,0},{2,1},{3,2},{5,4},{6,5},{7,6},{9,8},{10,9},{11,10},{13,12},{... | collective-permute-start | bytes 152 | tf_op jit(solution)/shard_map/ppermute | solution.py:32
  250.9 10.6 %collective-permute-start.1 = (f32[4,3]{1,0:T(4,128)S(1)}, f32[4,3]{1,0:T(4,128)S(1)}, u32[]{:S(2)}, u32[]{:S(2)}) collective-permute-start(f32[4,3]{1,0:T(4,128)S(1)} %get-tuple-element.277), channel_id=1, source_target_pairs={{0,1},{1,2},{2,3},{4,5},{5,6},{6,7},{8,9},{9,10},{10,11},{12,13},{... | collective-permute-start | bytes 152 | tf_op jit(solution)/shard_map/ppermute | solution.py:30
  257.3 5.0 %collective-permute-start.2 = (f32[64,3]{1,0:T(8,128)S(1)}, f32[64,3]{1,0:T(8,128)S(1)}, u32[]{:S(2)}, u32[]{:S(2)}) collective-permute-start(f32[64,3]{1,0:T(8,128)S(1)} %slice.1000), channel_id=1, source_target_pairs={{0,1},{1,2},{2,3},{4,5},{5,6},{6,7},{8,9},{9,10},{10,11},{12,13},{... | collective-permute-start | bytes 2312 | tf_op jit(solution)/shard_map/ppermute | solution.py:19
  287.5 5.9 %collective-permute-start.3 = (f32[4,3]{1,0:T(4,128)S(1)}, f32[4,3]{1,0:T(4,128)S(1)}, u32[]{:S(2)}, u32[]{:S(2)}) collective-permute-start(f32[4,3]{1,0:T(4,128)S(1)} %get-tuple-element.416), channel_id=1, source_target_pairs={{1,0},{2,1},{3,2},{5,4},{6,5},{7,6},{9,8},{10,9},{11,10},{13,12},{... | collective-permute-start | bytes 152 | tf_op jit(solution)/shard_map/ppermute | solution.py:32
  288.8 5.8 %collective-permute-start.4 = (f32[4,3]{1,0:T(4,128)S(1)}, f32[4,3]{1,0:T(4,128)S(1)}, u32[]{:S(2)}, u32[]{:S(2)}) collective-permute-start(f32[4,3]{1,0:T(4,128)S(1)} %get-tuple-element.417), channel_id=1, source_target_pairs={{0,1},{1,2},{2,3},{4,5},{5,6},{6,7},{8,9},{9,10},{10,11},{12,13},{... | collective-permute-start | bytes 152 | tf_op jit(solution)/shard_map/ppermute | solution.py:30
  320.0 5.9 %collective-permute-start.5 = (f32[4,3]{1,0:T(4,128)S(1)}, f32[4,3]{1,0:T(4,128)S(1)}, u32[]{:S(2)}, u32[]{:S(2)}) collective-permute-start(f32[4,3]{1,0:T(4,128)S(1)} %get-tuple-element.411), channel_id=1, source_target_pairs={{1,0},{2,1},{3,2},{5,4},{6,5},{7,6},{9,8},{10,9},{11,10},{13,12},{... | collective-permute-start | bytes 152 | tf_op jit(solution)/shard_map/ppermute | solution.py:32
  321.3 5.8 %collective-permute-start.6 = (f32[4,3]{1,0:T(4,128)S(1)}, f32[4,3]{1,0:T(4,128)S(1)}, u32[]{:S(2)}, u32[]{:S(2)}) collective-permute-start(f32[4,3]{1,0:T(4,128)S(1)} %get-tuple-element.412), channel_id=1, source_target_pairs={{0,1},{1,2},{2,3},{4,5},{5,6},{6,7},{8,9},{9,10},{10,11},{12,13},{... | collective-permute-start | bytes 152 | tf_op jit(solution)/shard_map/ppermute | solution.py:30
  352.5 5.9 %collective-permute-start.7 = (f32[4,3]{1,0:T(4,128)S(1)}, f32[4,3]{1,0:T(4,128)S(1)}, u32[]{:S(2)}, u32[]{:S(2)}) collective-permute-start(f32[4,3]{1,0:T(4,128)S(1)} %get-tuple-element.406), channel_id=1, source_target_pairs={{1,0},{2,1},{3,2},{5,4},{6,5},{7,6},{9,8},{10,9},{11,10},{13,12},{... | collective-permute-start | bytes 152 | tf_op jit(solution)/shard_map/ppermute | solution.py:32
  353.8 5.8 %collective-permute-start.8 = (f32[4,3]{1,0:T(4,128)S(1)}, f32[4,3]{1,0:T(4,128)S(1)}, u32[]{:S(2)}, u32[]{:S(2)}) collective-permute-start(f32[4,3]{1,0:T(4,128)S(1)} %get-tuple-element.407), channel_id=1, source_target_pairs={{0,1},{1,2},{2,3},{4,5},{5,6},{6,7},{8,9},{9,10},{10,11},{12,13},{... | collective-permute-start | bytes 152 | tf_op jit(solution)/shard_map/ppermute | solution.py:30
Sparse Core Ops, SparseCore 0:
  23.9 37.4 all-reduce.4
  164.6 28.8 reduce-scatter.1
  196.9 51.7 all-reduce.6
where the time goes:
time: 385 us; the launch traced here: 381 us
  waiting for transfers between devices  125 us (32%)
  blocking collectives  74.9 us (19%)
  matrix products  67.1 us (17%)
  local copies, waits for them, and re-layouts  45.6 us (12%)
  starting transfers between devices  27 us (7%)
  between operations  23.2 us (6%)
  other arithmetic  17.3 us (4%)
    psum x1, waiting for transfers between devices, body(): band = lax.psum(partial_band, 'src')  55.2 us
    dot_general x16, matrix products, add_block(): jnp.dot(feat, onehot, precision=lax.Precision.HIGHEST, preferred_element_...  51 us
    psum x4, blocking collectives, squares(): return lax.psum(jnp.sum(resid * resid), 'tm')  39.3 us
    psum x1, waiting for transfers between devices, body(): normals = lax.psum(own_normals, 'tm')  36.7 us
    psum x3, blocking collectives, body(): alpha = norm_now / lax.psum(jnp.sum(direction * image), 'tm')  35.7 us
    reduce_scatter x1, waiting for transfers between devices, body(): lax.psum_scatter(full_band, 'tm', scatter_dimension=1, tiled=True)  29 us
    another operation x3, local copies, waits for them, and re-layouts, knot_features(): return jnp.stack(rows, 0)  24.5 us
    ppermute x4, starting transfers between devices, with_halo(): lax.ppermute(tail, axis, [(i, (i + 1) % count) for i in range(ends)])  18.2 us
  transfers between devices with their start and end apart: 12, of which 7 were waited for; matrix products, arithmetic and copies ran while one was open for 1% of the time, Pallas kernels for 0%

commit v1 on v0

--- a/solution.py
+++ b/solution.py
@@ -216,7 +216,7 @@
     first = segment_of * KS + knot_start
     full_band = band_from(collect(features, first, knot_count), knot_count)
     partial_band = lax.psum_scatter(full_band, "tm", scatter_dimension=1, tiled=True)
-    band = lax.psum(partial_band, "src")
+    band = jnp.sum(lax.all_gather(partial_band, "src"), axis=0)
     matrix = band[:64]
     rhs = band[64:68]
     rim = from_behind(matrix[:, width - 3 :], "tm", 1)

time: 385 us -> 359 us (0.932)
  waiting for transfers between devices: 125 us -> 101 us
    psum x1 -> x0, waiting for transfers between devices: 55.2 us -> none  [body(): band = lax.psum(partial_band, 'src')]
    all_gather x0 -> x1, waiting for transfers between devices: none -> 29.8 us  [body(): band = jnp.sum(lax.all_gather(partial_band, 'src'), axis=0)]
  transfers between devices with their start and end apart: 12 -> 12, of which waited for: 7 -> 7; matrix products, arithmetic and copies ran while one was open for 1% -> 0% of each run, Pallas kernels for 0% -> 0%
where the time goes in v1:
time: 359 us; the launch traced here: 355 us
  waiting for transfers between devices  101 us (28%)
  blocking collectives  74.9 us (21%)
  matrix products  67.1 us (19%)
  local copies, waits for them, and re-layouts  42.5 us (12%)
  starting transfers between devices  27 us (8%)
  between operations  23.2 us (6%)
  other arithmetic  19.2 us (5%)
    dot_general x16, matrix products, add_block(): jnp.dot(feat, onehot, precision=lax.Precision.HIGHEST, preferred_element_...  51 us
    psum x4, blocking collectives, squares(): return lax.psum(jnp.sum(resid * resid), 'tm')  39.2 us
    psum x1, waiting for transfers between devices, body(): normals = lax.psum(own_normals, 'tm')  36.7 us
    psum x3, blocking collectives, body(): alpha = norm_now / lax.psum(jnp.sum(direction * image), 'tm')  35.7 us
    all_gather x1, waiting for transfers between devices, body(): band = jnp.sum(lax.all_gather(partial_band, 'src'), axis=0)  29.8 us
    reduce_scatter x1, waiting for transfers between devices, body(): lax.psum_scatter(full_band, 'tm', scatter_dimension=1, tiled=True)  29 us
    another operation x3, local copies, waits for them, and re-layouts, knot_features(): return jnp.stack(rows, 0)  24.5 us
    ppermute x4, starting transfers between devices, with_halo(): lax.ppermute(tail, axis, [(i, (i + 1) % count) for i in range(ends)])  18.2 us
  transfers between devices with their start and end apart: 12, of which 7 were waited for; matrix products, arithmetic and copies ran while one was open for 0% of the time, Pallas kernels for 0%

profile of v1, /device:TPU:0, one launch (start us, length us, event | category | flops | bytes accessed | tf_op | source)
XLA Modules:
  0.0 355.3 jit_solution(7119071215838263206)
XLA Ops:
  10.7 12.4 %while.34 = (s32[]{:T(128)}, f32[20,2048]{1,0:T(8,128)S(1)}, f32[8,20,512]{2,1,0:T(8,128)S(1)}, s32[8,512]{1,0:T(8,128)S(1)}, s32[]{:T(128)}, /*index=5*/s32[]{:T(128)}) while((s32[]{:T(128)}, f32[20,2048]{1,0:T(8,128)S(1)}, f32[8,20,512]{2,1,0:T(8,128)S(1)}, s32[8,512]{1,0:T(8,128)S(1)}, s32[]{:T(128)}, ...), condition=%wide.region_1.2_spmd.clone, body=%wide.region_0.1_spmd.clone.sunk | while | flops 252788736 | bytes 415831 | solution.py:89
  24.8 36.7 %all-reduce.4.cloned.1.call-done = f32[20,2048]{1,0:T(8,128)} async-done(((f32[20,2048]{1,0:T(8,128)}), f32[20,2048]{1,0:T(8,128)}) %all-reduce.4.cloned.1.call-update) | async-done | bytes 163856 | tf_op jit(solution)/shard_map/psum | solution.py:207
  65.8 16.3 %while.33 = (s32[]{:T(128)}, f32[8,5,512]{2,1,0:T(8,128)S(1)}, s32[8,512]{1,0:T(8,128)S(1)}, f32[5,2048]{1,0:T(8,128)S(1)}, s32[]{:T(128)}) while((s32[]{:T(128)}, f32[8,5,512]{2,1,0:T(8,128)S(1)}, s32[8,512]{1,0:T(8,128)S(1)}, f32[5,2048]{1,0:T(8,128)S(1)}, s32[]{:T(128)}) %tuple.351), condition=%wide.region_4.5_spmd.clone, body=%wide.region_3.4_spmd.clone.sunk | while | flops 63963136 | bytes 88133 | solution.py:139
  69.8 2.0 fusion.158
  71.9 2.0 fusion.158
  73.9 2.0 fusion.158
  78.0 2.0 fusion.158
  84.6 24.5 %stack.624 = f32[128,8,512]{2,0,1:T(8,128)} concatenate(f32[1,8,512]{2,0,1:T(1,128)S(1)} %bitcast.485, f32[1,8,512]{2,0,1:T(1,128)} %bitcast.536, f32[1,8,512]{2,0,1:T(1,128)} %bitcast.537, f32[1,8,512]{2,0,1:T(1,128)} %bitcast.538, f32[1,8,512]{2,0,1:T(1,128)S(1)} %bitcast.487, f32[1,8,512]{2,0,1:T(1,128)} %bitcast.539, f32[1,8,512]{2,0,1:T(1,128)} %bitcast.540, ...), dimensions={0} | concatenate | bytes 4194304 | tf_op jit(solution)/shard_map/stack | solution.py:66
  109.1 45.1 %while.35 = (s32[]{:T(128)}, f32[128,4096]{1,0:T(8,128)S(1)}, f32[8,128,512]{2,1,0:T(8,128)}, s32[8,512]{1,0:T(8,128)}, s32[]{:T(128)}, /*index=5*/s32[]{:T(128)}) while((s32[]{:T(128)}, f32[128,4096]{1,0:T(8,128)S(1)}, f32[8,128,512]{2,1,0:T(8,128)}, s32[8,512]{1,0:T(8,128)}, s32[]{:T(128)}, /*index=5*/s32[]{:T(128)}) %tuple.349), condition=%wide.region_7.8_spmd.clone, body=%wide.region_6.7_spmd.clone.sunk | while | flops 3224371200 | bytes 4463187 | solution.py:89
  109.8 4.9 %fusion.162 = f32[128,4096]{1,0:T(8,128)S(1)} fusion(s32[512]{0:T(512)S(1)} %bitcast.581, f32[128,4096]{1,0:T(8,128)S(1)} %get-tuple-element.605, pred[]{:T(512)S(6)} %compare.8, f32[8,128,512]{2,1,0:T(8,128)} %get-tuple-element.612, s32[]{:T(128)} %get-tuple-element.604), kind=kOutput, calls=%fused_computation.19.clone.1 | convolution fusion | flops 3224371200 | bytes 4459009 | tf_op jit(solution)/shard_map/while/body/eval_jaxpr/dot_general | solution.py:83
  115.4 4.9 %fusion.162 = f32[128,4096]{1,0:T(8,128)S(1)} fusion(s32[512]{0:T(512)S(1)} %bitcast.581, f32[128,4096]{1,0:T(8,128)S(1)} %get-tuple-element.605, pred[]{:T(512)S(6)} %compare.8, f32[8,128,512]{2,1,0:T(8,128)} %get-tuple-element.612, s32[]{:T(128)} %get-tuple-element.604), kind=kOutput, calls=%fused_computation.19.clone.1 | convolution fusion | flops 3224371200 | bytes 4459009 | tf_op jit(solution)/shard_map/while/body/eval_jaxpr/dot_general | solution.py:83
  121.1 4.9 %fusion.162 = f32[128,4096]{1,0:T(8,128)S(1)} fusion(s32[512]{0:T(512)S(1)} %bitcast.581, f32[128,4096]{1,0:T(8,128)S(1)} %get-tuple-element.605, pred[]{:T(512)S(6)} %compare.8, f32[8,128,512]{2,1,0:T(8,128)} %get-tuple-element.612, s32[]{:T(128)} %get-tuple-element.604), kind=kOutput, calls=%fused_computation.19.clone.1 | convolution fusion | flops 3224371200 | bytes 4459009 | tf_op jit(solution)/shard_map/while/body/eval_jaxpr/dot_general | solution.py:83
  126.7 4.9 %fusion.162 = f32[128,4096]{1,0:T(8,128)S(1)} fusion(s32[512]{0:T(512)S(1)} %bitcast.581, f32[128,4096]{1,0:T(8,128)S(1)} %get-tuple-element.605, pred[]{:T(512)S(6)} %compare.8, f32[8,128,512]{2,1,0:T(8,128)} %get-tuple-element.612, s32[]{:T(128)} %get-tuple-element.604), kind=kOutput, calls=%fused_computation.19.clone.1 | convolution fusion | flops 3224371200 | bytes 4459009 | tf_op jit(solution)/shard_map/while/body/eval_jaxpr/dot_general | solution.py:83
  132.3 4.9 %fusion.162 = f32[128,4096]{1,0:T(8,128)S(1)} fusion(s32[512]{0:T(512)S(1)} %bitcast.581, f32[128,4096]{1,0:T(8,128)S(1)} %get-tuple-element.605, pred[]{:T(512)S(6)} %compare.8, f32[8,128,512]{2,1,0:T(8,128)} %get-tuple-element.612, s32[]{:T(128)} %get-tuple-element.604), kind=kOutput, calls=%fused_computation.19.clone.1 | convolution fusion | flops 3224371200 | bytes 4459009 | tf_op jit(solution)/shard_map/while/body/eval_jaxpr/dot_general | solution.py:83
  137.9 4.9 %fusion.162 = f32[128,4096]{1,0:T(8,128)S(1)} fusion(s32[512]{0:T(512)S(1)} %bitcast.581, f32[128,4096]{1,0:T(8,128)S(1)} %get-tuple-element.605, pred[]{:T(512)S(6)} %compare.8, f32[8,128,512]{2,1,0:T(8,128)} %get-tuple-element.612, s32[]{:T(128)} %get-tuple-element.604), kind=kOutput, calls=%fused_computation.19.clone.1 | convolution fusion | flops 3224371200 | bytes 4459009 | tf_op jit(solution)/shard_map/while/body/eval_jaxpr/dot_general | solution.py:83
  143.5 4.9 %fusion.162 = f32[128,4096]{1,0:T(8,128)S(1)} fusion(s32[512]{0:T(512)S(1)} %bitcast.581, f32[128,4096]{1,0:T(8,128)S(1)} %get-tuple-element.605, pred[]{:T(512)S(6)} %compare.8, f32[8,128,512]{2,1,0:T(8,128)} %get-tuple-element.612, s32[]{:T(128)} %get-tuple-element.604), kind=kOutput, calls=%fused_computation.19.clone.1 | convolution fusion | flops 3224371200 | bytes 4459009 | tf_op jit(solution)/shard_map/while/body/eval_jaxpr/dot_general | solution.py:83
  149.1 4.9 %fusion.162 = f32[128,4096]{1,0:T(8,128)S(1)} fusion(s32[512]{0:T(512)S(1)} %bitcast.581, f32[128,4096]{1,0:T(8,128)S(1)} %get-tuple-element.605, pred[]{:T(512)S(6)} %compare.8, f32[8,128,512]{2,1,0:T(8,128)} %get-tuple-element.612, s32[]{:T(128)} %get-tuple-element.604), kind=kOutput, calls=%fused_computation.19.clone.1 | convolution fusion | flops 3224371200 | bytes 4459009 | tf_op jit(solution)/shard_map/while/body/eval_jaxpr/dot_general | solution.py:83
  157.2 7.2 %stack.625 = f32[68,4096]{1,0:T(8,128)} concatenate(f32[1,4096]{1,0:T(1,128)S(1)} %get-tuple-element.269, f32[1,4096]{1,0:T(1,128)S(1)} %get-tuple-element.268, f32[1,4096]{1,0:T(1,128)S(1)} %get-tuple-element.267, f32[1,4096]{1,0:T(1,128)S(1)} %get-tuple-element.266, f32[1,4096]{1,0:T(1,128)S(1)} %get-tuple-element.268, f32[1,4096]{1,0:T(1,128)S(1)} %get-tuple-element.265, ...), dimensions={0} | concatenate | bytes 2228224 | tf_op jit(solution)/shard_map/stack | solution.py:114
  164.5 29.0 %reduce-scatter.2.cloned.1.call-done = f32[68,1024]{1,0:T(8,128)} async-done(((f32[68,4096]{1,0:T(8,128)}), f32[68,1024]{1,0:T(8,128)}) %reduce-scatter.2.cloned.1.call-update) | async-done | bytes 278544 | tf_op jit(solution)/shard_map/reduce_scatter | solution.py:218
  193.5 29.8 %all-gather.4.cloned.1.call-done = f32[8,68,1024]{2,1,0:T(8,128)} async-done(((f32[1,68,1024]{2,1,0:T(8,128)}), f32[8,68,1024]{2,1,0:T(8,128)}) %all-gather.4.cloned.1.call-update) | async-done | bytes 2228240 | tf_op jit(solution)/shard_map/all_gather | solution.py:219
  226.7 4.5 %collective-permute-start.1 = (f32[4,3]{1,0:T(4,128)S(1)}, f32[4,3]{1,0:T(4,128)S(1)}, u32[]{:S(2)}, u32[]{:S(2)}) collective-permute-start(f32[4,3]{1,0:T(4,128)S(1)} %get-tuple-element.277), channel_id=1, source_target_pairs={{0,1},{1,2},{2,3},{4,5},{5,6},{6,7},{8,9},{9,10},{10,11},{12,13},{... | collective-permute-start | bytes 152 | tf_op jit(solution)/shard_map/ppermute | solution.py:30
  231.4 3.4 collective-permute-start.2
  237.3 11.7 %all-reduce.1 = (f32[]{:T(128)}, f32[]{:T(128)}) all-reduce(f32[]{:T(128)} %get-tuple-element.131, f32[]{:T(128)} %get-tuple-element.130), channel_id=1, replica_groups=mesh['src'=8,'tm'=4] {'tm'}, use_global_device_ids=true, to_apply=%region_11.12 | all-reduce | flops 2 | bytes 16 | tf_op jit(solution)/shard_map/psum | solution.py:226
  250.9 9.2 %psum.66 = f32[]{:T(128)} all-reduce(f32[]{:T(128)} %multiply_reduce_fusion.33), channel_id=1, replica_groups=mesh['src'=8,'tm'=4] {'tm'}, use_global_device_ids=true, to_apply=%region_15.16 | all-reduce | flops 1 | bytes 8 | tf_op jit(solution)/shard_map/psum | solution.py:226
  262.7 4.5 %collective-permute-start.4 = (f32[4,3]{1,0:T(4,128)S(1)}, f32[4,3]{1,0:T(4,128)S(1)}, u32[]{:S(2)}, u32[]{:S(2)}) collective-permute-start(f32[4,3]{1,0:T(4,128)S(1)} %get-tuple-element.417), channel_id=1, source_target_pairs={{0,1},{1,2},{2,3},{4,5},{5,6},{6,7},{8,9},{9,10},{10,11},{12,13},{... | collective-permute-start | bytes 152 | tf_op jit(solution)/shard_map/ppermute | solution.py:30
  269.7 11.9 %psum.67 = f32[]{:T(128)} all-reduce(f32[]{:T(128)} %get-tuple-element.162), channel_id=1, replica_groups=mesh['src'=8,'tm'=4] {'tm'}, use_global_device_ids=true, to_apply=%region_17.18 | all-reduce | flops 1 | bytes 8 | tf_op jit(solution)/shard_map/psum | solution.py:235
  283.5 9.2 %psum.68 = f32[]{:T(128)} all-reduce(f32[]{:T(128)} %get-tuple-element.160), channel_id=1, replica_groups=mesh['src'=8,'tm'=4] {'tm'}, use_global_device_ids=true, to_apply=%region_19.20 | all-reduce | flops 1 | bytes 8 | tf_op jit(solution)/shard_map/psum | solution.py:226
  295.3 4.5 %collective-permute-start.6 = (f32[4,3]{1,0:T(4,128)S(1)}, f32[4,3]{1,0:T(4,128)S(1)}, u32[]{:S(2)}, u32[]{:S(2)}) collective-permute-start(f32[4,3]{1,0:T(4,128)S(1)} %get-tuple-element.412), channel_id=1, source_target_pairs={{0,1},{1,2},{2,3},{4,5},{5,6},{6,7},{8,9},{9,10},{10,11},{12,13},{... | collective-permute-start | bytes 152 | tf_op jit(solution)/shard_map/ppermute | solution.py:30
  302.2 11.9 %psum.69 = f32[]{:T(128)} all-reduce(f32[]{:T(128)} %get-tuple-element.158), channel_id=1, replica_groups=mesh['src'=8,'tm'=4] {'tm'}, use_global_device_ids=true, to_apply=%region_21.22 | all-reduce | flops 1 | bytes 8 | tf_op jit(solution)/shard_map/psum | solution.py:235
  316.0 9.2 %psum.70 = f32[]{:T(128)} all-reduce(f32[]{:T(128)} %multiply_reduce_fusion.29), channel_id=1, replica_groups=mesh['src'=8,'tm'=4] {'tm'}, use_global_device_ids=true, to_apply=%region_23.24 | all-reduce | flops 1 | bytes 8 | tf_op jit(solution)/shard_map/psum | solution.py:226
  327.8 4.5 %collective-permute-start.8 = (f32[4,3]{1,0:T(4,128)S(1)}, f32[4,3]{1,0:T(4,128)S(1)}, u32[]{:S(2)}, u32[]{:S(2)}) collective-permute-start(f32[4,3]{1,0:T(4,128)S(1)} %get-tuple-element.407), channel_id=1, source_target_pairs={{0,1},{1,2},{2,3},{4,5},{5,6},{6,7},{8,9},{9,10},{10,11},{12,13},{... | collective-permute-start | bytes 152 | tf_op jit(solution)/shard_map/ppermute | solution.py:30
  334.8 12.0 %psum.71 = f32[]{:T(128)} all-reduce(f32[]{:T(128)} %fusion.71), channel_id=1, replica_groups=mesh['src'=8,'tm'=4] {'tm'}, use_global_device_ids=true, to_apply=%region_25.26 | all-reduce | flops 1 | bytes 8 | tf_op jit(solution)/shard_map/psum | solution.py:235
  (162 shorter events, 60.6 us)
Async XLA Ops:
  7.2 54.3 %all-reduce.4.cloned.1.call-start = ((), (), s32[]{:S(2)}) async-start(), calls=%async_computation.1 | async-start | bytes 393216 | tf_op jit(solution)/shard_map/psum | solution.py:207
  10.7 13.3 %copy-start.3 = (f32[4,4096]{1,0:T(4,128)S(1)}, f32[4,4096]{1,0:T(4,128)}, u32[]{:S(2)}) copy-start(f32[4,4096]{1,0:T(4,128)} %param.14) | copy-start | bytes 196612
  10.7 13.4 %copy-start.8 = (s32[4096,1]{0,1:T(1,128)S(1)}, s32[4096,1]{0,1:T(1,128)}, u32[]{:S(2)}) copy-start(s32[4096,1]{0,1:T(1,128)} %param.21) | copy-start | bytes 49156
  10.7 13.4 %copy-start.7 = (s32[4096]{0:T(1024)S(1)}, s32[4096]{0:T(1024)}, u32[]{:S(2)}) copy-start(s32[4096]{0:T(1024)} %param.20) | copy-start | bytes 49156
  23.1 0.7 copy-start.1
  23.8 169.7 %reduce-scatter.2.cloned.1.call-start = ((), (), s32[]{:S(2)}) async-start(), calls=%async_computation.2 | async-start | bytes 1474560 | tf_op jit(solution)/shard_map/reduce_scatter | solution.py:218
  65.7 16.3 %copy-start = (f32[5,4096]{1,0:T(8,128)S(1)}, f32[5,4096]{1,0:T(8,128)}, u32[]{:S(2)}) copy-start(f32[5,4096]{1,0:T(8,128)} %param.15) | copy-start | bytes 245764
  65.7 16.4 %copy-start.2 = (f32[4096]{0:T(1024)S(1)}, f32[4096]{0:T(1024)}, u32[]{:S(2)}) copy-start(f32[4096]{0:T(1024)} %param.17) | copy-start | bytes 49156
  65.7 16.4 %copy-start.5 = (f32[4096]{0:T(1024)S(1)}, f32[4096]{0:T(1024)}, u32[]{:S(2)}) copy-start(f32[4096]{0:T(1024)} %param.18) | copy-start | bytes 49156
  65.7 16.4 %copy-start.6 = (f32[4096]{0:T(1024)S(1)}, f32[4096]{0:T(1024)}, u32[]{:S(2)}) copy-start(f32[4096]{0:T(1024)} %param.16) | copy-start | bytes 49156
  82.0 1.6 copy-start.4
  164.5 58.8 %all-gather.4.cloned.1.call-start = ((), (), s32[]{:S(2)}) async-start(), calls=%async_computation.3 | async-start | bytes 2654208 | tf_op jit(solution)/shard_map/all_gather | solution.py:219
  225.4 9.4 %collective-permute-start = (f32[4,3]{1,0:T(4,128)S(1)}, f32[4,3]{1,0:T(4,128)S(1)}, u32[]{:S(2)}, u32[]{:S(2)}) collective-permute-start(f32[4,3]{1,0:T(4,128)S(1)} %get-tuple-element.276), channel_id=1, source_target_pairs={{1,0},{2,1},{3,2},{5,4},{6,5},{7,6},{9,8},{10,9},{11,10},{13,12},{... | collective-permute-start | bytes 152 | tf_op jit(solution)/shard_map/ppermute | solution.py:32
  226.7 8.1 %collective-permute-start.1 = (f32[4,3]{1,0:T(4,128)S(1)}, f32[4,3]{1,0:T(4,128)S(1)}, u32[]{:S(2)}, u32[]{:S(2)}) collective-permute-start(f32[4,3]{1,0:T(4,128)S(1)} %get-tuple-element.277), channel_id=1, source_target_pairs={{0,1},{1,2},{2,3},{4,5},{5,6},{6,7},{8,9},{9,10},{10,11},{12,13},{... | collective-permute-start | bytes 152 | tf_op jit(solution)/shard_map/ppermute | solution.py:30
  231.4 5.0 %collective-permute-start.2 = (f32[64,3]{1,0:T(8,128)S(1)}, f32[64,3]{1,0:T(8,128)S(1)}, u32[]{:S(2)}, u32[]{:S(2)}) collective-permute-start(f32[64,3]{1,0:T(8,128)S(1)} %slice.1000), channel_id=1, source_target_pairs={{0,1},{1,2},{2,3},{4,5},{5,6},{6,7},{8,9},{9,10},{10,11},{12,13},{... | collective-permute-start | bytes 2312 | tf_op jit(solution)/shard_map/ppermute | solution.py:19
  261.4 5.9 %collective-permute-start.3 = (f32[4,3]{1,0:T(4,128)S(1)}, f32[4,3]{1,0:T(4,128)S(1)}, u32[]{:S(2)}, u32[]{:S(2)}) collective-permute-start(f32[4,3]{1,0:T(4,128)S(1)} %get-tuple-element.416), channel_id=1, source_target_pairs={{1,0},{2,1},{3,2},{5,4},{6,5},{7,6},{9,8},{10,9},{11,10},{13,12},{... | collective-permute-start | bytes 152 | tf_op jit(solution)/shard_map/ppermute | solution.py:32
  262.7 5.8 %collective-permute-start.4 = (f32[4,3]{1,0:T(4,128)S(1)}, f32[4,3]{1,0:T(4,128)S(1)}, u32[]{:S(2)}, u32[]{:S(2)}) collective-permute-start(f32[4,3]{1,0:T(4,128)S(1)} %get-tuple-element.417), channel_id=1, source_target_pairs={{0,1},{1,2},{2,3},{4,5},{5,6},{6,7},{8,9},{9,10},{10,11},{12,13},{... | collective-permute-start | bytes 152 | tf_op jit(solution)/shard_map/ppermute | solution.py:30
  294.0 5.9 %collective-permute-start.5 = (f32[4,3]{1,0:T(4,128)S(1)}, f32[4,3]{1,0:T(4,128)S(1)}, u32[]{:S(2)}, u32[]{:S(2)}) collective-permute-start(f32[4,3]{1,0:T(4,128)S(1)} %get-tuple-element.411), channel_id=1, source_target_pairs={{1,0},{2,1},{3,2},{5,4},{6,5},{7,6},{9,8},{10,9},{11,10},{13,12},{... | collective-permute-start | bytes 152 | tf_op jit(solution)/shard_map/ppermute | solution.py:32
  295.3 5.8 %collective-permute-start.6 = (f32[4,3]{1,0:T(4,128)S(1)}, f32[4,3]{1,0:T(4,128)S(1)}, u32[]{:S(2)}, u32[]{:S(2)}) collective-permute-start(f32[4,3]{1,0:T(4,128)S(1)} %get-tuple-element.412), channel_id=1, source_target_pairs={{0,1},{1,2},{2,3},{4,5},{5,6},{6,7},{8,9},{9,10},{10,11},{12,13},{... | collective-permute-start | bytes 152 | tf_op jit(solution)/shard_map/ppermute | solution.py:30
  326.5 5.9 %collective-permute-start.7 = (f32[4,3]{1,0:T(4,128)S(1)}, f32[4,3]{1,0:T(4,128)S(1)}, u32[]{:S(2)}, u32[]{:S(2)}) collective-permute-start(f32[4,3]{1,0:T(4,128)S(1)} %get-tuple-element.406), channel_id=1, source_target_pairs={{1,0},{2,1},{3,2},{5,4},{6,5},{7,6},{9,8},{10,9},{11,10},{13,12},{... | collective-permute-start | bytes 152 | tf_op jit(solution)/shard_map/ppermute | solution.py:32
  327.8 5.8 %collective-permute-start.8 = (f32[4,3]{1,0:T(4,128)S(1)}, f32[4,3]{1,0:T(4,128)S(1)}, u32[]{:S(2)}, u32[]{:S(2)}) collective-permute-start(f32[4,3]{1,0:T(4,128)S(1)} %get-tuple-element.407), channel_id=1, source_target_pairs={{0,1},{1,2},{2,3},{4,5},{5,6},{6,7},{8,9},{9,10},{10,11},{12,13},{... | collective-permute-start | bytes 152 | tf_op jit(solution)/shard_map/ppermute | solution.py:30
Sparse Core Ops, SparseCore 0:
  23.9 37.4 all-reduce.3
  164.6 28.8 reduce-scatter.1
  195.6 27.7 all-gather.3
